TPU v7x, 128 devices: a whole 4x4x4 slice. The times are simulated.
128 devices in a mesh: src: 8 (over x, y_lo), snk: 16 (over z, y_hi, core).
Axes of the slice: x: 4, y: 4 (y_hi: 2, y_lo: 2; y = y_hi * 2 + y_lo), z: 4, core: 2. Of those that a mesh axis runs over, the one named last changes fastest.
Arguments:
- elementals: bfloat16 [32, 8, 2, 256, 256], P('snk', 'src'), may hold values from -0.25 to 0.25
- perambulators: float32 [8, 32, 2, 256, 256], P('src', 'snk'), may hold values from -0.25 to 0.25
- source_times: int32 [8], replicated, may hold values from 0 to 31, as said below
- pair_index: int32 [8, 2], replicated, may hold values from 0 to 7, as said below
Outputs:
- boxes: float32 [2, 8, 8, 32], P(None, None, 'src', 'snk')
- crossed: float32 [2, 8, 8, 32], P(None, None, 'src', 'snk')
Inputs may be any that keep to these rules, and one draw needn't show every extreme that they name: `source_times`: source times are distinct and always include the first and the last sink time. `pair_index`: each row names two different momenta, and every momentum is the first entry of exactly one row.
All inputs are finite; a program needn't handle non-finite values.
Results may differ from a plain program's by a relative error of at most 0.0088.
Values may be sent and summed in bfloat16 or wider, within the bound.
A program may use at most 128 MiB of HBM per device.

v0:
```python
import jax
import jax.numpy as jnp
from jax import lax
from jax.sharding import PartitionSpec as P


def contract(former, latter, form):
    return jnp.einsum(form, former, latter, preferred_element_type=jnp.float32)


def complex_product(former, latter, form, axis):
    former_real, former_imaginary = (former[..., 0, :, :], former[..., 1, :, :])
    latter_real, latter_imaginary = (latter[..., 0, :, :], latter[..., 1, :, :])
    product_real = contract(former_real, latter_real, form) - contract(
        former_imaginary, latter_imaginary, form
    )
    product_imaginary = contract(former_real, latter_imaginary, form) + contract(
        former_imaginary, latter_real, form
    )
    return jnp.stack([product_real, product_imaginary], axis=axis)


def conjugate_product(former, latter, form, axis):
    former_real, former_imaginary = (former[..., 0, :, :], former[..., 1, :, :])
    latter_real, latter_imaginary = (latter[..., 0, :, :], latter[..., 1, :, :])
    product_real = contract(former_real, latter_real, form) + contract(
        former_imaginary, latter_imaginary, form
    )
    product_imaginary = contract(former_imaginary, latter_real, form) - contract(
        former_real, latter_imaginary, form
    )
    return jnp.stack([product_real, product_imaginary], axis=axis)


def complex_times(former, latter):
    return jnp.stack(
        [
            former[0] * latter[0] - former[1] * latter[1],
            former[0] * latter[1] + former[1] * latter[0],
        ],
        axis=0,
    )


def diagrams(sink_chain, source_chain, first_mom, second_mom):
    table = conjugate_product(sink_chain, source_chain, "aij,cij->ac", 0)
    box_value = complex_times(table[:, first_mom, first_mom], table[:, second_mom, second_mom])
    box_value = box_value - complex_times(
        table[:, first_mom, second_mom], table[:, second_mom, first_mom]
    )
    sink_first = jnp.take(sink_chain, first_mom, axis=0)
    sink_second = jnp.take(sink_chain, second_mom, axis=0)
    source_first = jnp.take(source_chain, first_mom, axis=0)
    source_second = jnp.take(source_chain, second_mom, axis=0)
    loop_aa = conjugate_product(sink_first, source_first, "kij,klj->kil", -3).astype(jnp.bfloat16)
    loop_bb = conjugate_product(sink_second, source_second, "kij,klj->kil", -3).astype(jnp.bfloat16)
    loop_ab = conjugate_product(sink_first, source_second, "kij,klj->kil", -3).astype(jnp.bfloat16)
    loop_ba = conjugate_product(sink_second, source_first, "kij,klj->kil", -3).astype(jnp.bfloat16)
    cross_value = complex_product(loop_aa, loop_bb, "kij,kji->k", 0) - complex_product(
        loop_ab, loop_ba, "kij,kji->k", 0
    )
    return (box_value, cross_value)


def local(elementals, perambulators, source_times, pair_index):
    sink_count = elementals.shape[0]
    propagator = perambulators[0].astype(jnp.bfloat16)
    piece = lax.all_gather(elementals, "src", axis=1, tiled=True)
    chained = complex_product(piece, propagator, "tmij,tjk->tmik", -3).astype(jnp.bfloat16)
    slot = lax.axis_index("src")
    moment = lax.dynamic_index_in_dim(source_times, slot, 0, keepdims=False)
    owner = moment // sink_count
    offset = moment % sink_count
    chosen = lax.dynamic_index_in_dim(piece, offset, 0, keepdims=False)
    holder = lax.axis_index("snk") == owner
    masked = jnp.where(holder, chosen, jnp.zeros_like(chosen))
    source_phase = lax.psum(masked, "snk").astype(jnp.float32).astype(jnp.bfloat16)
    source_chain = complex_product(propagator, source_phase, "tij,mjk->tmik", -3).astype(
        jnp.bfloat16
    )
    first_mom = pair_index[:, 0]
    second_mom = pair_index[:, 1]
    box_list = []
    cross_list = []
    for sink in range(sink_count):
        box_value, cross_value = diagrams(chained[sink], source_chain[sink], first_mom, second_mom)
        box_list.append(box_value)
        cross_list.append(cross_value)
    box_all = jnp.stack(box_list, axis=-1)[:, :, None, :]
    cross_all = jnp.stack(cross_list, axis=-1)[:, :, None, :]
    return (box_all, cross_all)


def solution(mesh):
    return jax.shard_map(
        local,
        mesh=mesh,
        in_specs=(P("snk", "src", None, None, None), P("src", "snk", None, None, None), P(), P()),
        out_specs=(P(None, None, "src", "snk"), P(None, None, "src", "snk")),
        check_vma=False,
    )
```

profile of v0, /device:TPU:1, one launch (start us, length us, event | category | flops | bytes accessed | tf_op | source)
XLA Modules:
  0.0 422.8 jit_solution(14653739123311612199)
XLA Ops:
  13.3 89.3 %all-gather.2.cloned.1.call-done = bf16[2,8,2,256,256]{4,3,1,0,2:T(8,128)(2,1)} async-done(((bf16[2,1,2,256,256]{4,3,1,0,2:T(8,128)(2,1)}), bf16[2,8,2,256,256]{4,3,1,0,2:T(8,128)(2,1)}) %all-gather.2.cloned.1.call-update) | async-done | bytes 4194320 | tf_op jit(solution)/shard_map/all_gather | solution.py:68
  102.6 3.1 select_bitcast_fusion
  114.4 3.7 gather_fusion.14
  118.0 3.6 gather_fusion.12
  123.6 3.9 slice_bitcast_fusion.27
  129.3 2.8 broadcast_select_fusion.3
  132.1 121.6 %all-reduce.2.cloned.1.call-done = bf16[8,2,256,256]{3,2,0,1:T(8,128)(2,1)} async-done(((bf16[8,2,256,256]{3,2,0,1:T(8,128)(2,1)}), bf16[8,2,256,256]{3,2,0,1:T(8,128)(2,1)}) %all-reduce.2.cloned.1.call-update) | async-done | bytes 2097168 | tf_op jit(solution)/shard_map/psum | solution.py:77
  285.8 3.6 gather_fusion.11
  289.4 3.6 gather_fusion.15
  293.0 3.6 gather_fusion.13
  296.6 3.6 gather_fusion.9
  300.2 4.4 %broadcast_select_fusion.1 = (bf16[8,2,256,256]{2,3,1,0:T(8,128)(2,1)S(1)}, bf16[8,2,256,256]{2,3,1,0:T(8,128)(2,1)S(1)}, bf16[8,2,256,256]{2,3,1,0:T(8,128)(2,1)S(1)}, bf16[8,2,256,256]{2,3,1,0:T(8,128)(2,1)S(1)}) fusion(bf16[8,2,256,256]{2,3,1,0:T(8,128)(2,1)} %gather_fusion.11, pred[8]{0:T(512)(128)(4,1)S(1)} %get-tuple-element.41, ...), kind=kLoop, calls=%fused_computation.84 | loop fusion | flops 4194304 | bytes 16777232 | tf_op jit(solution)/shard_map/jit(_take)/select_n | solution.py:54
  335.2 2.9 copy.260
  338.1 3.8 fusion.41
  341.9 3.4 fusion.33
  345.4 2.9 copy.269
  348.2 4.0 fusion.34
  352.3 2.9 copy.288
  355.2 3.8 fusion.43
  359.0 3.4 fusion.35
  362.4 3.0 copy.297
  365.3 4.0 fusion.28
  369.4 2.9 copy.204
  372.2 3.5 fusion.37
  375.8 3.4 fusion.29
  379.2 2.9 copy.213
  382.1 4.0 fusion.30
  386.1 2.9 copy.232
  392.2 3.5 fusion.31
  395.6 2.9 copy.241
  400.0 4.9 %fusion.8 = (f32[8]{0:T(128)S(1)}, f32[8]{0:T(128)S(1)}, f32[8]{0:T(128)S(1)}, f32[8]{0:T(128)S(1)}) fusion(f32[8,256,256]{1,2,0:T(8,128)} %copy.260, bf16[8,256,256]{1,2,0:T(8,128)(2,1)} %fusion.41, f32[8,256,256]{1,2,0:T(8,128)} %copy.269, f32[8,256,256]{2,1,0:T(8,128)} %fusion.76, bf16[8,2,256,256]{2,3,1,0:T(8,128)(2,1)} %copy-done.11, ...), kind=kOutput, calls=%fused_computation.48 | convolution fusion | flops 274726912 | bytes 9437312 | tf_op jit(solution)/shard_map/kij,klj->kil/dot_general | solution.py:8
  406.5 2.8 fusion.12
  (177 shorter events, 91.0 us)
Async XLA Ops:
  7.2 5.9 %copy-start.43 = (f32[1,2,2,256,256]{4,3,2,1,0:T(8,128)S(1)}, f32[1,2,2,256,256]{4,3,2,1,0:T(8,128)}, u32[]{:S(2)}) copy-start(f32[1,2,2,256,256]{4,3,2,1,0:T(8,128)} %param.7) | copy-start | bytes 3145732
  7.2 6.0 %copy-start.44 = (s32[8,2]{0,1:T(2,128)S(1)}, s32[8,2]{0,1:T(2,128)}, u32[]{:S(2)}) copy-start(s32[8,2]{0,1:T(2,128)} %param.9) | copy-start | bytes 196
  7.2 95.4 %all-gather.2.cloned.1.call-start = ((), (), s32[]{:S(2)}) async-start(), calls=%async_computation | async-start | bytes 4718592 | tf_op jit(solution)/shard_map/all_gather | solution.py:68
  9.2 244.6 %all-reduce.2.cloned.1.call-start = ((), (), s32[]{:S(2)}) async-start(), calls=%async_computation.1 | async-start | bytes 4194304 | tf_op jit(solution)/shard_map/psum | solution.py:77
  123.6 3.9 copy-start.36
  123.6 3.9 copy-start.37
  123.6 5.0 %copy-start.38 = (bf16[8,2,256,256]{3,2,1,0:T(8,128)(2,1)S(1)}, bf16[8,2,256,256]{3,2,1,0:T(8,128)(2,1)}, u32[]{:S(2)}) copy-start(bf16[8,2,256,256]{3,2,1,0:T(8,128)(2,1)} %gather_fusion.12) | copy-start | bytes 6291460
  123.6 5.7 %copy-start.39 = (bf16[8,2,256,256]{3,2,1,0:T(8,128)(2,1)S(1)}, bf16[8,2,256,256]{3,2,1,0:T(8,128)(2,1)}, u32[]{:S(2)}) copy-start(bf16[8,2,256,256]{3,2,1,0:T(8,128)(2,1)} %gather_fusion.8) | copy-start | bytes 6291460
  258.7 3.0 copy-start.20
  300.2 4.4 %copy-start.16 = (bf16[8,2,256,256]{3,2,1,0:T(8,128)(2,1)S(1)}, bf16[8,2,256,256]{3,2,1,0:T(8,128)(2,1)}, u32[]{:S(2)}) copy-start(bf16[8,2,256,256]{3,2,1,0:T(8,128)(2,1)} %get-tuple-element.79) | copy-start | bytes 6291460
  304.6 10.7 %copy-start.11 = (bf16[8,2,256,256]{2,3,1,0:T(8,128)(2,1)}, bf16[8,2,256,256]{2,3,1,0:T(8,128)(2,1)S(1)}, u32[]{:S(2)}) copy-start(bf16[8,2,256,256]{2,3,1,0:T(8,128)(2,1)S(1)} %get-tuple-element.63) | copy-start | bytes 6291460
  304.6 25.2 %copy-start.5 = (bf16[8,2,256,256]{2,3,1,0:T(8,128)(2,1)}, bf16[8,2,256,256]{2,3,1,0:T(8,128)(2,1)S(1)}, u32[]{:S(2)}) copy-start(bf16[8,2,256,256]{2,3,1,0:T(8,128)(2,1)S(1)} %get-tuple-element.62) | copy-start | bytes 6291460
  304.6 27.0 %copy-start.2 = (bf16[8,2,256,256]{2,3,1,0:T(8,128)(2,1)}, bf16[8,2,256,256]{2,3,1,0:T(8,128)(2,1)S(1)}, u32[]{:S(2)}) copy-start(bf16[8,2,256,256]{2,3,1,0:T(8,128)(2,1)S(1)} %get-tuple-element.78) | copy-start | bytes 6291460
  304.6 28.8 %copy-start.8 = (bf16[8,2,256,256]{2,3,1,0:T(8,128)(2,1)}, bf16[8,2,256,256]{2,3,1,0:T(8,128)(2,1)S(1)}, u32[]{:S(2)}) copy-start(bf16[8,2,256,256]{2,3,1,0:T(8,128)(2,1)S(1)} %get-tuple-element.77) | copy-start | bytes 6291460
  305.1 3.1 copy-start
  338.1 3.8 copy-start.9
  338.1 3.8 copy-start.17
  355.2 3.8 copy-start.12
  355.2 3.8 copy-start.18
  372.2 3.5 copy-start.3
  372.2 3.5 copy-start.14
  389.0 3.2 copy-start.15
  400.0 4.9 %copy-start.1 = (bf16[8,2,256,256]{3,2,1,0:T(8,128)(2,1)S(1)}, bf16[8,2,256,256]{3,2,1,0:T(8,128)(2,1)}, u32[]{:S(2)}) copy-start(bf16[8,2,256,256]{3,2,1,0:T(8,128)(2,1)} %get-tuple-element.65) | copy-start | bytes 6291460
  400.0 5.0 %copy-start.10 = (bf16[8,2,256,256]{2,3,1,0:T(8,128)(2,1)S(1)}, bf16[8,2,256,256]{2,3,1,0:T(8,128)(2,1)}, u32[]{:S(2)}) copy-start(bf16[8,2,256,256]{2,3,1,0:T(8,128)(2,1)} %copy-done.8) | copy-start | bytes 6291460
  400.0 5.6 %copy-start.30 = (f32[8,256,256]{2,1,0:T(8,128)S(1)}, f32[8,256,256]{2,1,0:T(8,128)}, u32[]{:S(2)}) copy-start(f32[8,256,256]{2,1,0:T(8,128)} %fusion.73) | copy-start | bytes 6291460
  400.0 6.2 %copy-start.35 = (f32[8,256,256]{1,2,0:T(8,128)S(1)}, f32[8,256,256]{1,2,0:T(8,128)}, u32[]{:S(2)}) copy-start(f32[8,256,256]{1,2,0:T(8,128)} %copy.288) | copy-start | bytes 6291460
  400.0 6.4 %copy-start.42 = (bf16[8,256,256]{1,2,0:T(8,128)(2,1)S(1)}, bf16[8,256,256]{1,2,0:T(8,128)(2,1)}, u32[]{:S(2)}) copy-start(bf16[8,256,256]{1,2,0:T(8,128)(2,1)} %fusion.43) | copy-start | bytes 3145732
  406.5 3.5 copy-start.33
  406.5 4.1 copy-start.34
  406.5 4.3 %copy-start.41 = (bf16[8,256,256]{1,2,0:T(8,128)(2,1)S(1)}, bf16[8,256,256]{1,2,0:T(8,128)(2,1)}, u32[]{:S(2)}) copy-start(bf16[8,256,256]{1,2,0:T(8,128)(2,1)} %fusion.37) | copy-start | bytes 3145732
  410.8 2.9 copy-start.31
  410.8 3.5 copy-start.32
  (15 other events, 36.0 us)
Sparse Core Ops, SparseCore 0:
  9.7 92.8 all-gather.1
  105.8 147.8 all-reduce.1
where the time goes:
time: 424 us; the launch traced here: 423 us
  waiting for transfers between devices  211 us (50%)
  matrix products  97.9 us (23%)
  local copies, waits for them, and re-layouts  82 us (19%)
  between operations  17.2 us (4%)
  other arithmetic  14.6 us (3%)
    psum x1, waiting for transfers between devices, local(): lax.psum(masked, 'snk').astype(jnp.float32).astype(jnp.bfloat16)  122 us
    dot_general x48, matrix products, contract(): return jnp.einsum(form, former, latter, preferred_element_type=jnp.float32)  97.9 us
    all_gather x1, waiting for transfers between devices, local(): piece = lax.all_gather(elementals, 'src', axis=1, tiled=True)  89.3 us
    unnamed x100, local copies, waits for them, and re-layouts  36 us
    squeeze x5, local copies, waits for them, and re-layouts, conjugate_product(): latter_real, latter_imaginary = (latter[..., 0, :, :], latter[..., 1, :, :])  10.4 us
  transfers between devices with their start and end apart: 2, of which 2 were waited for; matrix products, arithmetic and copies ran while one was open for 6% of the time, Pallas kernels for 0%

commit v1 on v0

v1 whole, which is shorter than its diff:
```python
import functools

import jax
import jax.numpy as jnp
from jax import lax
from jax.experimental import pallas as pl
from jax.experimental.pallas import tpu as pltpu
from jax.sharding import PartitionSpec as P

BF = jnp.bfloat16
F32 = jnp.float32
MESH = pl.DeviceIdType.MESH
N = 256
G = 64
HM = (G + N) // 2
NN = (((1,), (0,)), ((), ()))
NT = (((1,), (1,)), ((), ()))
TN = (((0,), (0,)), ((), ()))


def mm(form, a, b):
    return lax.dot_general(a, b, form, preferred_element_type=F32)


def kernel(
    times,
    pairs,
    e_ref,
    p_ref,
    box_ref,
    cross_ref,
    ebuf,
    abuf,
    bsel,
    fbuf,
    pw,
    pleft,
    sb,
    rb,
    lb,
    lt,
    mb,
    mt,
    cacc,
    tab,
    e_send,
    e_recv,
    a_send,
    a_recv,
    b_send,
    b_recv,
    c_send,
    c_recv,
    k_send,
    k_recv,
):
    s = lax.axis_index("src")
    k = lax.axis_index("snk")
    x, yl = s // 2, s % 2
    z, yh, core = k // 4, (k // 2) % 2, k % 2
    s_par = x * 2 + (1 - yl)
    s_right = ((x + 1) % 4) * 2 + yl
    s_left = ((x + 3) % 4) * 2 + yl
    s_opp = ((x + 2) % 4) * 2 + yl

    def other(m):
        return (m // 2) * 2 + (1 - m % 2)

    right, left, ypar = (s_right, k), (s_left, k), (s_par, k)

    barrier = pltpu.get_barrier_semaphore()
    for d in range(1, 16):
        pl.semaphore_signal(barrier, 1, device_id=(s, (k + d) % 16), device_id_type=MESH)
    for d in range(1, 8):
        pl.semaphore_signal(barrier, 1, device_id=((s + d) % 8, k), device_id_type=MESH)
    pl.semaphore_wait(barrier, 22)

    def rows(ref, lo, hi):
        return ref.at[:, pl.ds(lo, hi - lo), :]

    def e_msg(t, j):
        own = e_ref.at[t, 0]
        table = [
            (own, s, G, N, ypar),
            (own, s, G, N, right),
            (own, s, G, N, left),
            (None, s_par, G, N, right),
            (None, s_par, G, N, left),
            (None, s_left, G, HM, right),
            (None, s_right, HM, N, left),
            (None, other(s_left), G, HM, right),
            (None, other(s_right), HM, N, left),
            (own, s, 0, G, right),
            (own, s, 0, G, left),
            (None, s_left, 0, G // 2, right),
            (None, s_right, G // 2, G, left),
            (own, s, 0, G, ypar),
            (None, s_left, 0, G, ypar),
            (None, s_right, 0, G, ypar),
            (None, s_opp, 0, G, ypar),
        ]
        src, m, lo, hi, dev = table[j]
        dst = ebuf.at[t, m]
        src = dst if src is None else src
        return pltpu.make_async_remote_copy(
            rows(src, lo, hi),
            rows(dst, lo, hi),
            e_send.at[t, j],
            e_recv.at[t, j],
            device_id=dev,
            device_id_type=MESH,
        )

    def go(t, *js):
        for j in js:
            e_msg(t, j).start()

    def got(t, *js):
        for j in js:
            e_msg(t, j).wait_recv()

    def chunk(q):
        return pl.ds(pl.multiple_of(q * 16, 16), 16)

    def a_msg(d):
        q = (k + d) % 16
        return pltpu.make_async_remote_copy(
            e_ref.at[:, 0, :, chunk(q), :],
            abuf.at[pl.ds(2 * k, 2)],
            a_send,
            a_recv,
            device_id=(s, q),
            device_id_type=MESH,
        )

    def b_msg(d):
        q = (s + d) % 8
        return pltpu.make_async_remote_copy(
            bsel.at[q],
            fbuf.at[s, :, chunk(k), :],
            b_send,
            b_recv,
            device_id=(q, k),
            device_id_type=MESH,
        )

    def snk(zz, hh, cc):
        return (zz * 2 + hh) * 2 + cc

    zr, zl, zo, hp = (z + 1) % 4, (z + 3) % 4, (z + 2) % 4, 1 - yh
    to_zr, to_zl = (s, snk(zr, yh, core)), (s, snk(zl, yh, core))
    to_hp, to_core = (s, snk(z, hp, core)), (s, snk(z, yh, 1 - core))

    def c_msg(j):
        table = [
            (snk(z, yh, core), 0, 8, to_hp),
            (snk(z, yh, core), 0, 8, to_zr),
            (snk(z, yh, core), 0, 8, to_zl),
            (snk(z, hp, core), 0, 8, to_zr),
            (snk(z, hp, core), 0, 8, to_zl),
            (snk(zl, yh, core), 0, 4, to_zr),
            (snk(zr, yh, core), 4, 8, to_zl),
            (snk(zl, hp, core), 0, 4, to_zr),
            (snk(zr, hp, core), 4, 8, to_zl),
        ]
        q, lo, hi, dev = table[j]
        ref = fbuf.at[pl.ds(lo, hi - lo), :, chunk(q), :]
        return pltpu.make_async_remote_copy(
            ref, ref, c_send.at[j], c_recv.at[j], device_id=dev, device_id_type=MESH
        )

    def k_msg(j):
        table = [(z, yh), (z, hp), (zl, yh), (zr, yh), (zl, hp), (zr, hp), (zo, yh), (zo, hp)]
        zz, hh = table[j]
        ref = fbuf.at[:, :, chunk(snk(zz, hh, core)), :]
        return pltpu.make_async_remote_copy(
            ref, ref, k_send.at[j], k_recv.at[j], device_id=to_core, device_id_type=MESH
        )

    def put_s(u, m, real, imaginary):
        real = real.astype(BF)
        sb[u, m, 0] = real
        sb[u, m, 1] = imaginary.astype(BF)
        sb[u, m, 2] = -real

    def sink_chain(u, m, ref):
        both = jnp.concatenate([ref[0], ref[1]], axis=1)
        put_s(u, m, mm(NN, both, pw[u, :, 0:N]), mm(NN, both, pw[u, :, N : 2 * N]))

    def source_chain(m):
        both = jnp.concatenate([fbuf[m, 0], fbuf[m, 1]], axis=0)
        out = mm(NN, pleft[...], both).astype(BF)
        for u in range(2):
            for c in range(2):
                rb[u, m, c] = out[(2 * u + c) * N : (2 * u + c + 1) * N]

    def loops(u, m):
        sr, si, sn = sb[u, m, 0], sb[u, m, 1], sb[u, m, 2]
        rr, ri = rb[u, m, 0], rb[u, m, 1]
        r_row = jnp.concatenate([rr, ri], axis=1)
        r_col = jnp.concatenate([rr, ri], axis=0)
        for c, (one, two) in enumerate(((sr, si), (si, sn))):
            out = mm(NT, jnp.concatenate([one, two], axis=1), r_row).astype(BF)
            lb[m, c] = out
            lt[m, c] = out.T
        for c, (one, two) in enumerate(((sr, si), (si, sn))):
            out = mm(TN, r_col, jnp.concatenate([one, two], axis=0)).astype(BF)
            mb[m, c] = out
            mt[m, c] = out.T

    def crossed(u):
        def pair(n, carry):
            a, b = pairs[n, 0], pairs[n, 1]

            def body(i, acc):
                re, im = acc
                r = pl.ds(pl.multiple_of(i * 16, 16), 16)
                for one, two, sign in ((lb, lt, 1.0), (mb, mt, -1.0)):
                    ar, ai = one[a, 0, r, :].astype(F32), one[a, 1, r, :].astype(F32)
                    br, bi = two[b, 0, r, :].astype(F32), two[b, 1, r, :].astype(F32)
                    if sign > 0:
                        re = re + (ar * br - ai * bi)
                        im = im + (ar * bi + ai * br)
                    else:
                        re = re - (ar * br - ai * bi)
                        im = im - (ar * bi + ai * br)
                return re, im

            zero = jnp.zeros((16, N), F32)
            sums = lax.fori_loop(0, 16, body, (zero, zero), unroll=4)
            for c in range(2):
                v = sums[c]
                v = v[0:8] + v[8:16]
                cacc[u, c, n] = v[:, 0:128] + v[:, 128:256]
            return carry

        lax.fori_loop(0, 8, pair, 0)

    def trace_table(u):
        def side(ref, i):
            r = pl.ds(i * 16, 16)
            return jnp.concatenate(
                [ref[u, :, c, r, :].reshape(128, N) for c in range(2)], axis=0
            )

        total = mm(
            NT,
            jnp.concatenate([side(sb, i) for i in range(16)], axis=1),
            jnp.concatenate([side(rb, i) for i in range(16)], axis=1),
        )
        real = total[0:128, 0:128] + total[128:256, 128:256]
        imaginary = total[128:256, 0:128] - total[0:128, 128:256]
        row = lax.broadcasted_iota(jnp.int32, (128, 128), 0) % 16
        col = lax.broadcasted_iota(jnp.int32, (128, 128), 1) % 16
        for c, part in enumerate((real, imaginary)):
            part = jnp.where(row == col, part, 0.0)
            tab[u, c] = jnp.sum(part.reshape(8, 16, 128), axis=1)

    def finish():
        sub = lax.broadcasted_iota(jnp.int32, (8, 128), 0)
        lane = lax.broadcasted_iota(jnp.int32, (8, 128), 1) // 16
        first = jnp.zeros((8, 128), jnp.int32)
        second = jnp.zeros((8, 128), jnp.int32)
        for n in range(8):
            first = jnp.where(sub == n, pairs[n, 0], first)
            second = jnp.where(sub == n, pairs[n, 1], second)

        def pick(table, one, two):
            got_rows = jnp.zeros((8, 128), F32)
            for m in range(8):
                got_rows = got_rows + jnp.where(one == m, table[m : m + 1, :], 0.0)
            return jnp.sum(jnp.where(lane == two, got_rows, 0.0), axis=1, keepdims=True)

        boxes, crosses = [], []
        for u in range(2):
            val = []
            for one, two in ((first, first), (second, second), (first, second), (second, first)):
                val.append([pick(tab[u, c], one, two) for c in range(2)])
            (ar, ai), (br, bi), (cr, ci), (dr, di) = val
            boxes.append(
                (
                    (ar * br - ai * bi) - (cr * dr - ci * di),
                    (ar * bi + ai * br) - (cr * di + ci * dr),
                )
            )
            crosses.append(
                [
                    jnp.sum(jnp.sum(cacc[u, c], axis=1), axis=1, keepdims=True)
                    for c in range(2)
                ]
            )
        for c in range(2):
            box_ref[c] = jnp.concatenate([boxes[0][c], boxes[1][c]], axis=1)
            cross_ref[c] = jnp.concatenate([crosses[0][c], crosses[1][c]], axis=1)

    for d in range(1, 16):
        a_msg(d).start()
    go(0, 0, 1, 2, 9, 10, 13)

    abuf[pl.ds(2 * k, 2)] = e_ref[:, 0, :, chunk(k), :]
    for u in range(2):
        real = p_ref[0, u, 0].astype(BF)
        imaginary = p_ref[0, u, 1].astype(BF)
        pw[u, 0:N, 0:N] = real
        pw[u, 0:N, N : 2 * N] = imaginary
        pw[u, N : 2 * N, 0:N] = -imaginary
        pw[u, N : 2 * N, N : 2 * N] = real
        base = 2 * u * N
        pleft[base : base + N, 0:N] = real
        pleft[base : base + N, N : 2 * N] = -imaginary
        pleft[base + N : base + 2 * N, 0:N] = imaginary
        pleft[base + N : base + 2 * N, N : 2 * N] = real
    for u in range(2):
        sink_chain(u, s, e_ref.at[u, 0])

    pltpu.make_async_copy(abuf.at[0:30], abuf.at[0:30], a_recv).wait()
    for n in range(8):
        bsel[n] = abuf[times[n]]
    for d in range(1, 8):
        b_msg(d).start()
    fbuf[s, :, chunk(k), :] = bsel[s]

    got(0, 0)
    go(0, 3, 4)
    pltpu.make_async_copy(bsel.at[0:7], bsel.at[0:7], b_recv).wait()
    for j in (0, 1, 2):
        c_msg(j).start()
    k_msg(0).start()
    got(0, 9)
    go(0, 11, 14)
    got(0, 10)
    go(0, 12, 15)
    got(0, 1)
    go(0, 5)
    got(0, 2)
    go(0, 6)
    go(1, 0, 1, 2, 9, 10, 13)
    c_msg(0).wait_recv()
    c_msg(3).start()
    c_msg(4).start()
    k_msg(1).start()
    got(0, 11, 12)
    go(0, 16)
    got(0, 3)
    go(0, 7)
    got(0, 4)
    go(0, 8)
    c_msg(1).wait_recv()
    c_msg(5).start()
    k_msg(2).start()
    c_msg(2).wait_recv()
    c_msg(6).start()
    k_msg(3).start()
    got(1, 0)
    go(1, 3, 4)
    c_msg(3).wait_recv()
    c_msg(7).start()
    k_msg(4).start()
    c_msg(4).wait_recv()
    c_msg(8).start()
    k_msg(5).start()
    got(1, 9)
    go(1, 11, 14)
    got(1, 10)
    go(1, 12, 15)
    c_msg(5).wait_recv()
    c_msg(6).wait_recv()
    k_msg(6).start()
    c_msg(7).wait_recv()
    c_msg(8).wait_recv()
    k_msg(7).start()
    got(0, 13, 14, 15, 16, 5, 6, 7, 8)
    for j in range(8):
        k_msg(j).wait_recv()

    def place(j):
        dx = jnp.where(j // 2 == 1, 3, jnp.where(j // 2 == 2, 1, jnp.where(j // 2 == 3, 2, 0)))
        return ((x + dx) % 4) * 2 + (yl + j % 2) % 2

    @pl.loop(0, 8)
    def _(j):
        m = place(j)

        @pl.when(j == 1)
        def _():
            got(1, 1)
            go(1, 5)

        @pl.when(j == 2)
        def _():
            got(1, 2)
            go(1, 6)

        @pl.when(j == 3)
        def _():
            got(1, 11, 12)
            go(1, 16)

        @pl.when(j == 4)
        def _():
            got(1, 3)
            go(1, 7)

        @pl.when(j == 5)
        def _():
            got(1, 4)
            go(1, 8)

        source_chain(m)

        @pl.when(j > 0)
        def _():
            sink_chain(0, m, ebuf.at[0, m])

        loops(0, m)

    crossed(0)
    trace_table(0)

    @pl.loop(0, 8)
    def _(j):
        m = place(j)

        @pl.when(j == 1)
        def _():
            got(1, 13)

        @pl.when(j == 3)
        def _():
            got(1, 14)

        @pl.when(j == 5)
        def _():
            got(1, 15)

        @pl.when(j == 6)
        def _():
            got(1, 5, 6)

        @pl.when(j == 7)
        def _():
            got(1, 7, 8, 16)

        @pl.when(j > 0)
        def _():
            sink_chain(1, m, ebuf.at[1, m])

        loops(1, m)

    crossed(1)
    trace_table(1)
    finish()

    pltpu.make_async_copy(abuf.at[0:30], abuf.at[0:30], a_send).wait()
    pltpu.make_async_copy(bsel.at[0:7], bsel.at[0:7], b_send).wait()
    for t in range(2):
        for j in range(17):
            e_msg(t, j).wait_send()
    for j in range(9):
        c_msg(j).wait_send()
    for j in range(8):
        k_msg(j).wait_send()


def local(elementals, perambulators, source_times, pair_index):
    vm = pl.BlockSpec(memory_space=pltpu.VMEM)
    sm = pl.BlockSpec(memory_space=pltpu.SMEM)
    dma = pltpu.SemaphoreType.DMA
    boxes, crossed = pl.pallas_call(
        kernel,
        out_shape=(
            jax.ShapeDtypeStruct((2, 8, 2), F32),
            jax.ShapeDtypeStruct((2, 8, 2), F32),
        ),
        in_specs=[sm, sm, vm, vm],
        out_specs=(vm, vm),
        scratch_shapes=[
            pltpu.VMEM((2, 8, 2, N, N), BF),
            pltpu.VMEM((32, 2, 16, N), BF),
            pltpu.VMEM((8, 2, 16, N), BF),
            pltpu.VMEM((8, 2, N, N), BF),
            pltpu.VMEM((2, 2 * N, 2 * N), BF),
            pltpu.VMEM((4 * N, 2 * N), BF),
            pltpu.VMEM((2, 8, 3, N, N), BF),
            pltpu.VMEM((2, 8, 2, N, N), BF),
            pltpu.VMEM((8, 2, N, N), BF),
            pltpu.VMEM((8, 2, N, N), BF),
            pltpu.VMEM((8, 2, N, N), BF),
            pltpu.VMEM((8, 2, N, N), BF),
            pltpu.VMEM((2, 2, 8, 8, 128), F32),
            pltpu.VMEM((2, 2, 8, 128), F32),
            dma((2, 17)),
            dma((2, 17)),
            dma,
            dma,
            dma,
            dma,
            dma((9,)),
            dma((9,)),
            dma((8,)),
            dma((8,)),
        ],
        compiler_params=pltpu.CompilerParams(
            collective_id=0, has_side_effects=True, vmem_limit_bytes=56 * 1024 * 1024
        ),
        name="diagrams",
    )(source_times, pair_index, elementals, perambulators)
    return boxes[:, :, None, :], crossed[:, :, None, :]


def solution(mesh):
    return jax.shard_map(
        local,
        mesh=mesh,
        in_specs=(P("snk", "src", None, None, None), P("src", "snk", None, None, None), P(), P()),
        out_specs=(P(None, None, "src", "snk"), P(None, None, "src", "snk")),
        check_vma=False,
    )
```

time: 424 us -> 68.7 us (0.16)
  waiting for transfers between devices: 211 us -> 0 us
  matrix products: 97.9 us -> 0 us
  local copies, waits for them, and re-layouts: 82 us -> 3.36 us
  Pallas kernels: 0 us -> 64.5 us
  between operations: 17.2 us -> 0.65 us
  other arithmetic: 14.6 us -> 0 us
    psum x1 -> x0, waiting for transfers between devices: 122 us -> none  [local(): lax.psum(masked, 'snk').astype(jnp.float32).astype(jnp.bfloat16)]
    dot_general x48 -> x0, matrix products: 97.9 us -> none  [contract(): return jnp.einsum(form, former, latter, preferred_element_type=jnp.float32)]
    all_gather x1 -> x0, waiting for transfers between devices: 89.3 us -> none  [local(): piece = lax.all_gather(elementals, 'src', axis=1, tiled=True)]
    pallas_call x0 -> x1, Pallas kernels: none -> 64.5 us  [local(): pl.pallas_call(kernel, out_shape=(jax.ShapeDtypeStruct((2, 8, 2), F32), j...]
    unnamed x100 -> x5, local copies, waits for them, and re-layouts: 36 us -> 3.36 us
    gather x16 -> x0, local copies, waits for them, and re-layouts: 30.2 us -> none  [the longest x2 7.21 us: diagrams(): source_first = jnp.take(source_chain, first_mom, axis=0)]
    squeeze x6 -> x0, local copies, waits for them, and re-layouts: 14.3 us -> none  [the longest x5 10.4 us: conjugate_product(): latter_real, latter_imaginary = (latter[..., 0, :, :], latter[..., 1, :, :])]
    select_n x3 -> x0, other arithmetic: 10.3 us -> none  [the longest x1 4.39 us: diagrams(): source_second = jnp.take(source_chain, second_mom, axis=0)]
  transfers between devices with their start and end apart: 2 -> 0, of which waited for: 2 -> 0; matrix products, arithmetic and copies ran while one was open for 6% -> 0% of each run, Pallas kernels for 0% -> 0%
where the time goes in v1:
time: 68.7 us; the launch traced here: 68.5 us
  Pallas kernels  64.5 us (94%)
  local copies, waits for them, and re-layouts  3.36 us (5%)
    pallas_call x1, Pallas kernels, local(): pl.pallas_call(kernel, out_shape=(jax.ShapeDtypeStruct((2, 8, 2), F32), j...  64.5 us
    unnamed x5, local copies, waits for them, and re-layouts  3.36 us

profile of v1, /device:TPU:1, one launch (start us, length us, event | category | flops | bytes accessed | tf_op | source)
XLA Modules:
  0.0 68.5 jit_solution(9961308678921783741)
XLA Ops:
  0.6 1.3 %copy.6.pairs = s32[8,2]{1,0:T(8,128)} copy(s32[8,2]{0,1:T(2,128)} %param.7) | data formatting | bytes 128 | tf_op args[3]
  2.0 64.5 %diagrams.1 = (f32[2,8,2]{2,1,0:T(8,128)}, f32[2,8,2]{2,1,0:T(8,128)}) custom-call(s32[8]{0:T(128)} %times.1, s32[8,2]{1,0:T(8,128)} %copy.6.pairs, bf16[2,1,2,256,256]{4,3,2,1,0:T(8,128)(2,1)} %e_ref.1, f32[1,2,2,256,256]{4,3,2,1,0:T(8,128)} %p_ref.1), custom_call_target="tpu_custom_call" | custom-call | tf_op jit(solution)/shard_map/diagrams/pallas_call | solution.py:469
  66.5 0.0 copy-start
  66.5 1.4 %copy.9 = f32[2,8,1,2]{1,3,2,0:T(2,128)} copy(f32[2,8,1,2]{3,1,0,2:T(8,128)} %bitcast.3) | data formatting | bytes 256
  67.9 0.0 copy-done
  67.9 0.7 copy.10
Async XLA Ops:
  66.5 1.4 %copy-start = (f32[2,8,2]{2,1,0:T(8,128)S(1)}, f32[2,8,2]{2,1,0:T(8,128)}, u32[]{:S(2)}) copy-start(f32[2,8,2]{2,1,0:T(8,128)} %get-tuple-element.5) | copy-start | bytes 388

commit v2 on v0

v2 whole, which is shorter than its diff:
```python
import functools

import jax
import jax.numpy as jnp
from jax import lax
from jax.experimental import pallas as pl
from jax.experimental.pallas import tpu as pltpu
from jax.sharding import PartitionSpec as P

BF = jnp.bfloat16
F32 = jnp.float32
MESH = pl.DeviceIdType.MESH
N = 256
G = 80
GM, HM = 32, 176
NN = (((1,), (0,)), ((), ()))
NT = (((1,), (1,)), ((), ()))
TN = (((0,), (0,)), ((), ()))


def mm(form, a, b):
    return lax.dot_general(a, b, form, preferred_element_type=F32)


def kernel(
    times,
    pairs,
    e_in,
    p_in,
    box_ref,
    cross_ref,
    ebuf,
    pbuf,
    abuf_r,
    abuf_i,
    bsel,
    fbuf,
    pw,
    ph,
    vb,
    lb,
    lt,
    mb,
    mt,
    cacc,
    tab,
    in_sem,
    e_send,
    e_recv,
    a_send,
    a_recv,
    b_send,
    b_recv,
    c_send,
    c_recv,
    k_send,
    k_recv,
):
    abuf = (abuf_r, abuf_i)
    s = lax.axis_index("src")
    k = lax.axis_index("snk")
    x, yl = s // 2, s % 2
    z, yh, core = k // 4, (k // 2) % 2, k % 2
    s_par = x * 2 + (1 - yl)
    s_right = ((x + 1) % 4) * 2 + yl
    s_left = ((x + 3) % 4) * 2 + yl
    s_opp = ((x + 2) % 4) * 2 + yl

    def other(m):
        return (m // 2) * 2 + (1 - m % 2)

    right, left, ypar = (s_right, k), (s_left, k), (s_par, k)

    khp = (z * 2 + (1 - yh)) * 2 + core

    barrier = pltpu.get_barrier_semaphore()
    for d in range(1, 16):
        pl.semaphore_signal(barrier, 1, device_id=(s, (k + d) % 16), device_id_type=MESH)
    for d in range(1, 8):
        for q in (k, khp):
            pl.semaphore_signal(barrier, 1, device_id=((s + d) % 8, q), device_id_type=MESH)

    def in_copy(n):
        if n < 2:
            return pltpu.make_async_copy(e_in.at[n, 0], ebuf.at[n, s], in_sem.at[n])
        return pltpu.make_async_copy(p_in.at[0], pbuf, in_sem.at[2])

    for n in range(3):
        in_copy(n).start()
    in_copy(0).wait()
    in_copy(1).wait()
    pl.semaphore_wait(barrier, 29)

    def rows(ref, lo, hi):
        return ref.at[:, pl.ds(lo, hi - lo), :]

    def e_msg(t, j):
        own = ebuf.at[t, s]
        table = [
            (own, s, G, N, ypar),
            (own, s, G, N, right),
            (own, s, G, N, left),
            (None, s_par, G, N, right),
            (None, s_par, G, N, left),
            (None, s_left, G, HM, right),
            (None, s_right, HM, N, left),
            (None, other(s_left), G, HM, right),
            (None, other(s_right), HM, N, left),
            (own, s, 0, G, right),
            (own, s, 0, G, left),
            (None, s_left, 0, GM, right),
            (None, s_right, GM, G, left),
            (own, s, 0, G, ypar),
            (None, s_left, 0, G, ypar),
            (None, s_right, 0, G, ypar),
            (None, s_opp, 0, G, ypar),
        ]
        src, m, lo, hi, dev = table[j]
        dst = ebuf.at[t, m]
        src = dst if src is None else src
        return pltpu.make_async_remote_copy(
            rows(src, lo, hi),
            rows(dst, lo, hi),
            e_send.at[t, j],
            e_recv.at[t, j],
            device_id=dev,
            device_id_type=MESH,
        )

    def go(t, *js):
        for j in js:
            e_msg(t, j).start()

    def got(t, *js):
        for j in js:
            e_msg(t, j).wait_recv()

    def place_of(q):
        return (q % 2) * 8 + q // 2

    def chunk(q):
        return pl.ds(pl.multiple_of(place_of(q) * 16, 16), 16)

    def chunks(zz, cc):
        return pl.ds(pl.multiple_of(cc * 128 + zz * 32, 32), 32)

    def a_msg(h, d):
        q = (k + d) % 16
        return pltpu.make_async_remote_copy(
            ebuf.at[:, s, h, chunk(q), :],
            abuf[h].at[pl.ds(2 * k, 2)],
            a_send.at[h],
            a_recv.at[h],
            device_id=(s, q),
            device_id_type=MESH,
        )

    def b_msg(h, d, far):
        q = (s + d) % 8
        return pltpu.make_async_remote_copy(
            bsel.at[h, q],
            fbuf.at[s, h, chunk(k), :],
            b_send.at[h],
            b_recv.at[h],
            device_id=(q, khp if far else k),
            device_id_type=MESH,
        )

    zr, zl, zo = (z + 1) % 4, (z + 3) % 4, (z + 2) % 4
    to_zr, to_zl = (s, (zr * 2 + yh) * 2 + core), (s, (zl * 2 + yh) * 2 + core)
    to_core = (s, (z * 2 + yh) * 2 + 1 - core)

    def c_msg(h, j):
        zz, lo, dev = [
            (z, 0, to_zr),
            (z, 4, to_zl),
            (z, 4, to_zr),
            (z, 0, to_zl),
            (zl, 0, to_zr),
            (zr, 4, to_zl),
        ][j]
        ref = fbuf.at[pl.ds(lo, 4), h, chunks(zz, core), :]
        return pltpu.make_async_remote_copy(
            ref, ref, c_send.at[h, j], c_recv.at[h, j], device_id=dev, device_id_type=MESH
        )

    def k_msg(h, j):
        zz, lo, count = [(z, 0, 8), (zl, 0, 8), (zr, 0, 8), (zo, 0, 4), (zo, 4, 4)][j]
        ref = fbuf.at[pl.ds(lo, count), h, chunks(zz, core), :]
        return pltpu.make_async_remote_copy(
            ref, ref, k_send.at[h, j], k_recv.at[h, j], device_id=to_core, device_id_type=MESH
        )

    def chain(u, *ms):
        lhs = jnp.concatenate(
            [jnp.concatenate([ebuf[u, m, 0], ebuf[u, m, 1]], axis=1) for m in ms], axis=0
        )
        out = mm(NN, lhs, pw[u]).astype(BF)
        rhs = [
            jnp.concatenate([out[i * N : (i + 1) * N, c * N : (c + 1) * N] for c in range(2)], axis=0)
            for i in range(len(ms))
        ]
        out = mm(NN, ph[u], jnp.concatenate(rhs, axis=1)).astype(BF)
        for i, m in enumerate(ms):
            real, imaginary = (out[c * N : (c + 1) * N, i * N : (i + 1) * N] for c in range(2))
            vb[u, m, 0] = real
            vb[u, m, 1] = imaginary
            vb[u, m, 2] = -real

    def loops(u, m):
        vr, vi, vn = vb[u, m, 0], vb[u, m, 1], vb[u, m, 2]
        fr, fi = fbuf[m, 0], fbuf[m, 1]
        f_row = jnp.concatenate([fr, fi], axis=1)
        f_col = jnp.concatenate([fr, fi], axis=0)
        for c, (one, two) in enumerate(((vr, vi), (vi, vn))):
            out = mm(NT, jnp.concatenate([one, two], axis=1), f_row).astype(BF)
            lb[u, m, c] = out
            lt[u, m, c] = out.T
        for c, (one, two) in enumerate(((vr, vi), (vi, vn))):
            out = mm(TN, f_col, jnp.concatenate([one, two], axis=0)).astype(BF)
            mb[u, m, c] = out
            mt[u, m, c] = out.T

    def crossed(u, n):
        a, b = pairs[0, n], pairs[1, n]
        re = jnp.zeros((16, N), F32)
        im = jnp.zeros((16, N), F32)
        for i in range(16):
            r = pl.ds(i * 16, 16)
            for one, two, sign in ((lb, lt, 1.0), (mb, mt, -1.0)):
                ar, ai = one[u, a, 0, r, :].astype(F32), one[u, a, 1, r, :].astype(F32)
                br, bi = two[u, b, 0, r, :].astype(F32), two[u, b, 1, r, :].astype(F32)
                if sign > 0:
                    re = re + (ar * br - ai * bi)
                    im = im + (ar * bi + ai * br)
                else:
                    re = re - (ar * br - ai * bi)
                    im = im - (ar * bi + ai * br)
        for c, v in enumerate((re, im)):
            v = v[0:8] + v[8:16]
            cacc[u, c, n] = v[:, 0:128] + v[:, 128:256]

    def trace_table(u):
        def side(ref, i):
            r = pl.ds(i * 16, 16)
            return jnp.concatenate([ref[:, c, r, :].reshape(128, N) for c in range(2)], axis=0)

        total = mm(
            NT,
            jnp.concatenate([side(vb.at[u], i) for i in range(16)], axis=1),
            jnp.concatenate([side(fbuf, i) for i in range(16)], axis=1),
        )
        real = total[0:128, 0:128] + total[128:256, 128:256]
        imaginary = total[128:256, 0:128] - total[0:128, 128:256]
        row = lax.broadcasted_iota(jnp.int32, (128, 128), 0) % 16
        col = lax.broadcasted_iota(jnp.int32, (128, 128), 1) % 16
        for c, part in enumerate((real, imaginary)):
            part = jnp.where(row == col, part, 0.0)
            tab[u, c] = jnp.sum(part.reshape(8, 16, 128), axis=1)

    def finish():
        sub = lax.broadcasted_iota(jnp.int32, (8, 128), 0)
        lane = lax.broadcasted_iota(jnp.int32, (8, 128), 1) // 16
        first = jnp.zeros((8, 128), jnp.int32)
        second = jnp.zeros((8, 128), jnp.int32)
        for n in range(8):
            first = jnp.where(sub == n, pairs[0, n], first)
            second = jnp.where(sub == n, pairs[1, n], second)

        def pick(table, one, two):
            got_rows = jnp.zeros((8, 128), F32)
            for m in range(8):
                got_rows = got_rows + jnp.where(one == m, table[m : m + 1, :], 0.0)
            return jnp.sum(jnp.where(lane == two, got_rows, 0.0), axis=1, keepdims=True)

        spot = lax.broadcasted_iota(jnp.int32, (8, 128), 1) == sub

        def along(column):
            return jnp.sum(jnp.where(spot, column, 0.0), axis=0, keepdims=True)[:, 0:8]

        for u in range(2):
            val = []
            for one, two in ((first, first), (second, second), (first, second), (second, first)):
                val.append([pick(tab[u, c], one, two) for c in range(2)])
            (ar, ai), (br, bi), (cr, ci), (dr, di) = val
            box = (
                (ar * br - ai * bi) - (cr * dr - ci * di),
                (ar * bi + ai * br) - (cr * di + ci * dr),
            )
            for c in range(2):
                cross = jnp.sum(jnp.sum(cacc[u, c], axis=1), axis=1, keepdims=True)
                box_ref[c, u : u + 1, :] = along(box[c])
                cross_ref[c, u : u + 1, :] = along(cross)

    def all_of(sem, count):
        ref = abuf_r.at[pl.ds(0, count)]
        return pltpu.make_async_copy(ref, ref, sem)

    a_all = [all_of(a_recv.at[h], 30) for h in range(2)]
    a_out = [all_of(a_send.at[h], 30) for h in range(2)]
    b_all = [all_of(b_recv.at[h], 15) for h in range(2)]
    b_out = [all_of(b_send.at[h], 15) for h in range(2)]

    def choose(h):
        abuf[h][pl.ds(2 * k, 2)] = ebuf[:, s, h, chunk(k), :]
        a_all[h].wait()
        for n in range(8):
            bsel[h, n] = abuf[h][times[n]]
        for d in range(1, 8):
            b_msg(h, d, True).start()
            b_msg(h, d, False).start()
        b_msg(h, 0, True).start()
        fbuf[s, h, chunk(k), :] = bsel[h, s]

    def spread(h):
        b_all[h].wait()
        for j in (0, 1, 2, 3):
            c_msg(h, j).start()
        k_msg(h, 0).start()

    def c_got(h, j):
        c_msg(h, j).wait_recv()

    for h in range(2):
        for d in range(1, 16):
            a_msg(h, d).start()
    go(0, 9, 10)
    go(1, 9, 10)
    go(0, 1, 2)

    in_copy(2).wait()
    for u in range(2):
        real = pbuf[u, 0].astype(BF)
        imaginary = pbuf[u, 1].astype(BF)
        pw[u, 0:N, 0:N] = real
        pw[u, 0:N, N : 2 * N] = imaginary
        pw[u, N : 2 * N, 0:N] = -imaginary
        pw[u, N : 2 * N, N : 2 * N] = real
        ph[u, 0:N, 0:N] = real.T
        ph[u, 0:N, N : 2 * N] = imaginary.T
        ph[u, N : 2 * N, 0:N] = (-imaginary).T
        ph[u, N : 2 * N, N : 2 * N] = real.T

    choose(0)
    got(0, 9, 10)
    go(0, 11, 12)
    got(1, 9, 10)
    go(1, 11, 12)
    go(0, 0)
    choose(1)
    go(1, 1, 2)
    got(0, 1)
    go(0, 5)
    got(0, 2)
    go(0, 6)
    go(0, 13, 14, 15)
    go(1, 0)
    spread(0)
    chain(0, s, s_left, s_right)
    got(0, 0)
    go(0, 3, 4)
    got(0, 11, 12)
    go(0, 16)
    spread(1)
    got(1, 1)
    go(1, 5)
    got(1, 2)
    go(1, 6)
    c_got(0, 0)
    c_msg(0, 4).start()
    c_got(0, 1)
    c_msg(0, 5).start()
    c_got(0, 2)
    k_msg(0, 1).start()
    c_got(0, 3)
    k_msg(0, 2).start()
    chain(1, s, s_left, s_right)
    got(1, 0)
    go(1, 3, 4)
    c_got(1, 0)
    c_msg(1, 4).start()
    c_got(1, 1)
    c_msg(1, 5).start()
    c_got(1, 2)
    k_msg(1, 1).start()
    c_got(1, 3)
    k_msg(1, 2).start()
    got(0, 3)
    go(0, 7)
    got(0, 4)
    go(0, 8)
    go(1, 13, 14, 15)
    got(1, 11, 12)
    go(1, 16)
    c_got(0, 4)
    k_msg(0, 3).start()
    c_got(0, 5)
    k_msg(0, 4).start()
    got(0, 13)
    got(0, 5, 6)
    chain(0, s_par, s_opp)
    c_got(1, 4)
    k_msg(1, 3).start()
    c_got(1, 5)
    k_msg(1, 4).start()
    got(0, 14, 15)
    chain(0, other(s_left), other(s_right))
    got(1, 3)
    go(1, 7)
    got(1, 4)
    go(1, 8)
    for h in range(2):
        for j in range(5):
            k_msg(h, j).wait_recv()

    def place(j):
        q = j % 4
        dx = jnp.where(q == 1, 3, jnp.where(q == 2, 1, jnp.where(q == 3, 2, 0)))
        return ((x + dx) % 4) * 2 + (yl + j // 4) % 2

    for j in range(4):
        loops(0, place(j))
    got(0, 7, 8, 16)
    chain(0, other(s_opp))
    for j in range(4, 8):
        loops(0, place(j))
    trace_table(0)
    got(1, 5, 6)
    got(1, 13)
    chain(1, s_opp, s_par)
    for j in range(4):
        loops(1, place(j))
        crossed(0, j)
    got(1, 14, 15)
    chain(1, other(s_left), other(s_right))
    for j in range(4, 7):
        loops(1, place(j))
        crossed(0, j)
    got(1, 7, 8, 16)
    chain(1, other(s_opp))
    loops(1, place(7))
    crossed(0, 7)
    trace_table(1)

    @pl.loop(0, 8)
    def _(n):
        crossed(1, n)

    finish()

    for h in range(2):
        a_out[h].wait()
        b_out[h].wait()
    for t in range(2):
        for j in range(17):
            e_msg(t, j).wait_send()
    for h in range(2):
        for j in range(6):
            c_msg(h, j).wait_send()
        for j in range(5):
            k_msg(h, j).wait_send()


def local(elementals, perambulators, source_times, pair_index):
    vm = pl.BlockSpec(memory_space=pltpu.VMEM)
    sm = pl.BlockSpec(memory_space=pltpu.SMEM)
    hbm = pl.BlockSpec(memory_space=pl.ANY)
    dma = pltpu.SemaphoreType.DMA
    boxes, crossed = pl.pallas_call(
        kernel,
        out_shape=(
            jax.ShapeDtypeStruct((2, 2, 8), F32),
            jax.ShapeDtypeStruct((2, 2, 8), F32),
        ),
        in_specs=[sm, sm, hbm, hbm],
        out_specs=(vm, vm),
        scratch_shapes=[
            pltpu.VMEM((2, 8, 2, N, N), BF),
            pltpu.VMEM((2, 2, N, N), F32),
            pltpu.VMEM((32, 16, N), BF),
            pltpu.VMEM((32, 16, N), BF),
            pltpu.VMEM((2, 8, 16, N), BF),
            pltpu.VMEM((8, 2, N, N), BF),
            pltpu.VMEM((2, 2 * N, 2 * N), BF),
            pltpu.VMEM((2, 2 * N, 2 * N), BF),
            pltpu.VMEM((2, 8, 3, N, N), BF),
            pltpu.VMEM((2, 8, 2, N, N), BF),
            pltpu.VMEM((2, 8, 2, N, N), BF),
            pltpu.VMEM((2, 8, 2, N, N), BF),
            pltpu.VMEM((2, 8, 2, N, N), BF),
            pltpu.VMEM((2, 2, 8, 8, 128), F32),
            pltpu.VMEM((2, 2, 8, 128), F32),
            dma((3,)),
            dma((2, 17)),
            dma((2, 17)),
            dma((2,)),
            dma((2,)),
            dma((2,)),
            dma((2,)),
            dma((2, 6)),
            dma((2, 6)),
            dma((2, 5)),
            dma((2, 5)),
        ],
        compiler_params=pltpu.CompilerParams(
            collective_id=0, has_side_effects=True, vmem_limit_bytes=56 * 1024 * 1024
        ),
        name="diagrams",
    )(source_times, pair_index.T, elementals, perambulators)
    return tuple(v.transpose(0, 2, 1)[:, :, None, :] for v in (boxes, crossed))


def solution(mesh):
    return jax.shard_map(
        local,
        mesh=mesh,
        in_specs=(P("snk", "src", None, None, None), P("src", "snk", None, None, None), P(), P()),
        out_specs=(P(None, None, "src", "snk"), P(None, None, "src", "snk")),
        check_vma=False,
    )
```

time: 424 us -> 59 us (0.14)
  waiting for transfers between devices: 211 us -> 0 us
  matrix products: 97.9 us -> 0 us
  local copies, waits for them, and re-layouts: 82 us -> 1.89 us
  Pallas kernels: 0 us -> 56.3 us
  between operations: 17.2 us -> 0.65 us
  other arithmetic: 14.6 us -> 0 us
    psum x1 -> x0, waiting for transfers between devices: 122 us -> none  [local(): lax.psum(masked, 'snk').astype(jnp.float32).astype(jnp.bfloat16)]
    dot_general x48 -> x0, matrix products: 97.9 us -> none  [contract(): return jnp.einsum(form, former, latter, preferred_element_type=jnp.float32)]
    all_gather x1 -> x0, waiting for transfers between devices: 89.3 us -> none  [local(): piece = lax.all_gather(elementals, 'src', axis=1, tiled=True)]
    pallas_call x0 -> x1, Pallas kernels: none -> 56.3 us  [local(): pl.pallas_call(kernel, out_shape=(jax.ShapeDtypeStruct((2, 2, 8), F32), j...]
    unnamed x100 -> x6, local copies, waits for them, and re-layouts: 36 us -> 1.89 us
    gather x16 -> x0, local copies, waits for them, and re-layouts: 30.2 us -> none  [the longest x2 7.21 us: diagrams(): source_first = jnp.take(source_chain, first_mom, axis=0)]
    squeeze x6 -> x0, local copies, waits for them, and re-layouts: 14.3 us -> none  [the longest x5 10.4 us: conjugate_product(): latter_real, latter_imaginary = (latter[..., 0, :, :], latter[..., 1, :, :])]
    select_n x3 -> x0, other arithmetic: 10.3 us -> none  [the longest x1 4.39 us: diagrams(): source_second = jnp.take(source_chain, second_mom, axis=0)]
  transfers between devices with their start and end apart: 2 -> 0, of which waited for: 2 -> 0; matrix products, arithmetic and copies ran while one was open for 6% -> 0% of each run, Pallas kernels for 0% -> 0%
where the time goes in v2:
time: 59 us; the launch traced here: 58.8 us
  Pallas kernels  56.3 us (95%)
  local copies, waits for them, and re-layouts  1.89 us (3%)
  between operations  0.65 us (1%)
    pallas_call x1, Pallas kernels, local(): pl.pallas_call(kernel, out_shape=(jax.ShapeDtypeStruct((2, 2, 8), F32), j...  56.3 us
    unnamed x6, local copies, waits for them, and re-layouts  1.89 us

profile of v2, /device:TPU:1, one launch (start us, length us, event | category | flops | bytes accessed | tf_op | source)
XLA Modules:
  0.0 58.8 jit_solution(11807200333468120871)
XLA Ops:
  0.6 56.3 %diagrams.1 = (f32[2,2,8]{2,1,0:T(2,128)}, f32[2,2,8]{2,1,0:T(2,128)}) custom-call(s32[8]{0:T(128)} %times.1, s32[2,8]{1,0:T(2,128)} %bitcast.13, bf16[2,1,2,256,256]{4,3,2,1,0:T(8,128)(2,1)} %e_in.1, f32[1,2,2,256,256]{4,3,2,1,0:T(8,128)} %p_in.1), custom_call_target="tpu_custom_call" | custom-call | tf_op jit(solution)/shard_map/diagrams/pallas_call | solution.py:469
  56.9 0.0 copy-start.1
  56.9 0.7 %copy-done.1 = f32[2,2,8]{2,1,0:T(2,128)S(1)} copy-done((f32[2,2,8]{2,1,0:T(2,128)S(1)}, f32[2,2,8]{2,1,0:T(2,128)}, u32[]{:S(2)}) %copy-start.1) | copy-done | bytes 152
  57.6 0.0 copy-start
  57.6 0.6 copy.10
  58.2 0.1 copy-done
  58.2 0.6 copy.11
Async XLA Ops:
  56.9 0.7 %copy-start.1 = (f32[2,2,8]{2,1,0:T(2,128)S(1)}, f32[2,2,8]{2,1,0:T(2,128)}, u32[]{:S(2)}) copy-start(f32[2,2,8]{2,1,0:T(2,128)} %get-tuple-element.4) | copy-start | bytes 388
  57.6 0.7 %copy-start = (f32[2,2,8]{2,1,0:T(2,128)S(1)}, f32[2,2,8]{2,1,0:T(2,128)}, u32[]{:S(2)}) copy-start(f32[2,2,8]{2,1,0:T(2,128)} %get-tuple-element.5) | copy-start | bytes 388

commit v3 on v2

--- a/solution.py
+++ b/solution.py
@@ -97,11 +97,11 @@
     def e_msg(t, j):
         own = ebuf.at[t, s]
         table = [
-            (own, s, G, N, ypar),
-            (own, s, G, N, right),
-            (own, s, G, N, left),
-            (None, s_par, G, N, right),
-            (None, s_par, G, N, left),
+            (own, s, G, HM, ypar),
+            (own, s, G, HM, right),
+            (own, s, HM, N, left),
+            (None, s_par, G, HM, right),
+            (None, s_par, HM, N, left),
             (None, s_left, G, HM, right),
             (None, s_right, HM, N, left),
             (None, other(s_left), G, HM, right),
@@ -114,6 +114,11 @@
             (None, s_left, 0, G, ypar),
             (None, s_right, 0, G, ypar),
             (None, s_opp, 0, G, ypar),
+            (own, s, HM, N, right),
+            (own, s, G, HM, left),
+            (None, s_par, HM, N, right),
+            (None, s_par, G, HM, left),
+            (own, s, HM, N, ypar),
         ]
         src, m, lo, hi, dev = table[j]
         dst = ebuf.at[t, m]
@@ -321,138 +326,172 @@
     def c_got(h, j):
         c_msg(h, j).wait_recv()
 
-    for h in range(2):
+    def chunks_out(h):
         for d in range(1, 16):
             a_msg(h, d).start()
-    go(0, 9, 10)
-    go(1, 9, 10)
+
+    def prepare():
+        in_copy(2).wait()
+        for u in range(2):
+            real = pbuf[u, 0].astype(BF)
+            imaginary = pbuf[u, 1].astype(BF)
+            pw[u, 0:N, 0:N] = real
+            pw[u, 0:N, N : 2 * N] = imaginary
+            pw[u, N : 2 * N, 0:N] = -imaginary
+            pw[u, N : 2 * N, N : 2 * N] = real
+            ph[u, 0:N, 0:N] = real.T
+            ph[u, 0:N, N : 2 * N] = imaginary.T
+            ph[u, N : 2 * N, 0:N] = (-imaginary).T
+            ph[u, N : 2 * N, N : 2 * N] = real.T
+
+    chunks_out(0)
+    chunks_out(1)
     go(0, 1, 2)
-
-    in_copy(2).wait()
-    for u in range(2):
-        real = pbuf[u, 0].astype(BF)
-        imaginary = pbuf[u, 1].astype(BF)
-        pw[u, 0:N, 0:N] = real
-        pw[u, 0:N, N : 2 * N] = imaginary
-        pw[u, N : 2 * N, 0:N] = -imaginary
-        pw[u, N : 2 * N, N : 2 * N] = real
-        ph[u, 0:N, 0:N] = real.T
-        ph[u, 0:N, N : 2 * N] = imaginary.T
-        ph[u, N : 2 * N, 0:N] = (-imaginary).T
-        ph[u, N : 2 * N, N : 2 * N] = real.T
-
-    choose(0)
-    got(0, 9, 10)
-    go(0, 11, 12)
-    got(1, 9, 10)
-    go(1, 11, 12)
-    go(0, 0)
-    choose(1)
     go(1, 1, 2)
+    prepare()
+    go(0, 13)
+    got(0, 2)
+    go(0, 6)
     got(0, 1)
     go(0, 5)
-    got(0, 2)
-    go(0, 6)
-    go(0, 13, 14, 15)
-    go(1, 0)
-    spread(0)
-    chain(0, s, s_left, s_right)
-    got(0, 0)
-    go(0, 3, 4)
-    got(0, 11, 12)
-    go(0, 16)
-    spread(1)
+    got(1, 2)
+    go(1, 6)
+    choose(0)
     got(1, 1)
     go(1, 5)
-    got(1, 2)
-    go(1, 6)
-    c_got(0, 0)
+    choose(1)
+    go(1, 13)
+    go(1, 0)
+    go(1, 9, 10)
+    go(0, 9, 10)
+    spread(0)
+    go(1, 21)
+    go(0, 21)
+    go(0, 0)
+    go(0, 17, 18)
+    go(1, 17, 18)
+    got(1, 10)
+    go(1, 12)
+    go(1, 15)
+    got(1, 9)
+    go(1, 11)
+    go(1, 14)
+    spread(1)
+    c_msg(0, 0).wait_recv()
     c_msg(0, 4).start()
-    c_got(0, 1)
+    c_msg(0, 1).wait_recv()
     c_msg(0, 5).start()
-    c_got(0, 2)
+    got(0, 10)
+    go(0, 15)
+    go(0, 12)
+    got(1, 0)
+    go(1, 3, 20)
+    got(0, 9)
+    go(0, 14)
+    go(0, 11)
+    c_msg(0, 3).wait_recv()
+    k_msg(0, 2).start()
+    c_msg(0, 2).wait_recv()
     k_msg(0, 1).start()
-    c_got(0, 3)
-    k_msg(0, 2).start()
+    got(1, 21)
+    go(1, 4, 19)
+    got(0, 17, 18)
+    chain(0, s, s_left, s_right)
+    c_msg(1, 0).wait_recv()
+    c_msg(1, 4).start()
+    c_msg(1, 1).wait_recv()
+    c_msg(1, 5).start()
+    got(0, 21)
+    go(0, 4, 19)
+    got(1, 17, 18)
     chain(1, s, s_left, s_right)
-    got(1, 0)
-    go(1, 3, 4)
-    c_got(1, 0)
-    c_msg(1, 4).start()
-    c_got(1, 1)
-    c_msg(1, 5).start()
-    c_got(1, 2)
+    got(1, 13, 5, 6, 11, 12)
+    chain(1, s_par, s_opp)
+    c_msg(0, 4).wait_recv()
+    k_msg(0, 3).start()
+    c_msg(0, 5).wait_recv()
+    k_msg(0, 4).start()
+    got(0, 0)
+    go(0, 3, 20)
+    c_msg(1, 2).wait_recv()
     k_msg(1, 1).start()
-    c_got(1, 3)
+    c_msg(1, 3).wait_recv()
     k_msg(1, 2).start()
+    go(1, 16)
+    got(1, 3)
+    go(1, 7)
+    c_msg(1, 4).wait_recv()
+    k_msg(1, 3).start()
+    c_msg(1, 5).wait_recv()
+    k_msg(1, 4).start()
+    got(0, 13, 5, 6, 11, 12)
+    chain(0, s_par, s_opp)
+    go(0, 16)
+    k_msg(0, 0).wait_recv()
+    k_msg(0, 1).wait_recv()
+    k_msg(0, 2).wait_recv()
+    k_msg(0, 3).wait_recv()
+    k_msg(0, 4).wait_recv()
+    k_msg(1, 0).wait_recv()
+    k_msg(1, 1).wait_recv()
+    k_msg(1, 2).wait_recv()
+    k_msg(1, 3).wait_recv()
+    k_msg(1, 4).wait_recv()
+    loops(1, s)
+    loops(1, s_left)
+    loops(1, s_right)
+    loops(0, s)
+    loops(0, s_left)
+    loops(0, s_right)
+    got(1, 4)
+    go(1, 8)
+    got(1, 19, 14, 20, 15)
+    chain(1, other(s_left), other(s_right))
+    got(0, 4)
+    go(0, 8)
+    loops(0, s_par)
+    loops(0, s_opp)
     got(0, 3)
     go(0, 7)
-    got(0, 4)
-    go(0, 8)
-    go(1, 13, 14, 15)
-    got(1, 11, 12)
-    go(1, 16)
-    c_got(0, 4)
-    k_msg(0, 3).start()
-    c_got(0, 5)
-    k_msg(0, 4).start()
-    got(0, 13)
-    got(0, 5, 6)
-    chain(0, s_par, s_opp)
-    c_got(1, 4)
-    k_msg(1, 3).start()
-    c_got(1, 5)
-    k_msg(1, 4).start()
-    got(0, 14, 15)
+    loops(1, s_par)
+    loops(1, s_opp)
+    got(0, 19, 14, 20, 15)
     chain(0, other(s_left), other(s_right))
-    got(1, 3)
-    go(1, 7)
-    got(1, 4)
-    go(1, 8)
-    for h in range(2):
-        for j in range(5):
-            k_msg(h, j).wait_recv()
-
-    def place(j):
-        q = j % 4
-        dx = jnp.where(q == 1, 3, jnp.where(q == 2, 1, jnp.where(q == 3, 2, 0)))
-        return ((x + dx) % 4) * 2 + (yl + j // 4) % 2
-
-    for j in range(4):
-        loops(0, place(j))
+    loops(0, other(s_left))
+    loops(0, other(s_right))
+    got(1, 7, 8, 16)
+    chain(1, other(s_opp))
+    loops(1, other(s_opp))
+    loops(1, other(s_left))
+    loops(1, other(s_right))
     got(0, 7, 8, 16)
     chain(0, other(s_opp))
-    for j in range(4, 8):
-        loops(0, place(j))
     trace_table(0)
-    got(1, 5, 6)
-    got(1, 13)
-    chain(1, s_opp, s_par)
-    for j in range(4):
-        loops(1, place(j))
-        crossed(0, j)
-    got(1, 14, 15)
-    chain(1, other(s_left), other(s_right))
-    for j in range(4, 7):
-        loops(1, place(j))
-        crossed(0, j)
-    got(1, 7, 8, 16)
-    chain(1, other(s_opp))
-    loops(1, place(7))
+    loops(0, other(s_opp))
+    crossed(0, 0)
+    crossed(0, 1)
+    crossed(0, 2)
+    crossed(0, 3)
+    crossed(0, 4)
+    crossed(0, 5)
+    crossed(0, 6)
     crossed(0, 7)
     trace_table(1)
-
-    @pl.loop(0, 8)
-    def _(n):
-        crossed(1, n)
-
+    crossed(1, 0)
+    crossed(1, 1)
+    crossed(1, 2)
+    crossed(1, 3)
+    crossed(1, 4)
+    crossed(1, 5)
+    crossed(1, 6)
+    crossed(1, 7)
     finish()
 
     for h in range(2):
         a_out[h].wait()
         b_out[h].wait()
     for t in range(2):
-        for j in range(17):
+        for j in range(22):
             e_msg(t, j).wait_send()
     for h in range(2):
         for j in range(6):
@@ -491,8 +530,8 @@
             pltpu.VMEM((2, 2, 8, 8, 128), F32),
             pltpu.VMEM((2, 2, 8, 128), F32),
             dma((3,)),
-            dma((2, 17)),
-            dma((2, 17)),
+            dma((2, 22)),
+            dma((2, 22)),
             dma((2,)),
             dma((2,)),
             dma((2,)),

time: 59 us -> 54.9 us (0.931)
  Pallas kernels: 56.3 us -> 52.2 us
    pallas_call x1, Pallas kernels: 56.3 us -> 52.2 us  [local(): pl.pallas_call(kernel, out_shape=(jax.ShapeDtypeStruct((2, 2, 8), F32), j...]
where the time goes in v3:
time: 54.9 us; the launch traced here: 54.7 us
  Pallas kernels  52.2 us (95%)
  local copies, waits for them, and re-layouts  1.89 us (3%)
  between operations  0.65 us (1%)
    pallas_call x1, Pallas kernels, local(): pl.pallas_call(kernel, out_shape=(jax.ShapeDtypeStruct((2, 2, 8), F32), j...  52.2 us
    unnamed x6, local copies, waits for them, and re-layouts  1.89 us

profile of v3, /device:TPU:1, one launch (start us, length us, event | category | flops | bytes accessed | tf_op | source)
XLA Modules:
  0.0 54.7 jit_solution(1664299207760631007)
XLA Ops:
  0.6 52.2 %diagrams.1 = (f32[2,2,8]{2,1,0:T(2,128)}, f32[2,2,8]{2,1,0:T(2,128)}) custom-call(s32[8]{0:T(128)} %times.1, s32[2,8]{1,0:T(2,128)} %bitcast.13, bf16[2,1,2,256,256]{4,3,2,1,0:T(8,128)(2,1)} %e_in.1, f32[1,2,2,256,256]{4,3,2,1,0:T(8,128)} %p_in.1), custom_call_target="tpu_custom_call" | custom-call | tf_op jit(solution)/shard_map/diagrams/pallas_call | solution.py:508
  52.8 0.0 copy-start.1
  52.9 0.7 %copy-done.1 = f32[2,2,8]{2,1,0:T(2,128)S(1)} copy-done((f32[2,2,8]{2,1,0:T(2,128)S(1)}, f32[2,2,8]{2,1,0:T(2,128)}, u32[]{:S(2)}) %copy-start.1) | copy-done | bytes 152
  53.5 0.0 copy-start
  53.5 0.6 %copy.10 = f32[2,8,1,2]{1,3,2,0:T(2,128)} copy(f32[2,8,1,2]{1,3,2,0:T(2,128)S(1)} %bitcast.12) | data formatting | bytes 256
  54.1 0.1 copy-done
  54.2 0.6 %copy.11 = f32[2,8,1,2]{1,3,2,0:T(2,128)} copy(f32[2,8,1,2]{1,3,2,0:T(2,128)S(1)} %bitcast.11) | data formatting | bytes 256
Async XLA Ops:
  52.8 0.7 %copy-start.1 = (f32[2,2,8]{2,1,0:T(2,128)S(1)}, f32[2,2,8]{2,1,0:T(2,128)}, u32[]{:S(2)}) copy-start(f32[2,2,8]{2,1,0:T(2,128)} %get-tuple-element.4) | copy-start | bytes 388
  53.5 0.7 %copy-start = (f32[2,2,8]{2,1,0:T(2,128)S(1)}, f32[2,2,8]{2,1,0:T(2,128)}, u32[]{:S(2)}) copy-start(f32[2,2,8]{2,1,0:T(2,128)} %get-tuple-element.5) | copy-start | bytes 388

commit v4 on v3

--- a/solution.py
+++ b/solution.py
@@ -27,8 +27,7 @@
     pairs,
     e_in,
     p_in,
-    box_ref,
-    cross_ref,
+    out_ref,
     ebuf,
     pbuf,
     abuf_r,
@@ -263,7 +262,7 @@
             part = jnp.where(row == col, part, 0.0)
             tab[u, c] = jnp.sum(part.reshape(8, 16, 128), axis=1)
 
-    def finish():
+    def finish(u):
         sub = lax.broadcasted_iota(jnp.int32, (8, 128), 0)
         lane = lax.broadcasted_iota(jnp.int32, (8, 128), 1) // 16
         first = jnp.zeros((8, 128), jnp.int32)
@@ -283,19 +282,18 @@
         def along(column):
             return jnp.sum(jnp.where(spot, column, 0.0), axis=0, keepdims=True)[:, 0:8]
 
-        for u in range(2):
-            val = []
-            for one, two in ((first, first), (second, second), (first, second), (second, first)):
-                val.append([pick(tab[u, c], one, two) for c in range(2)])
-            (ar, ai), (br, bi), (cr, ci), (dr, di) = val
-            box = (
-                (ar * br - ai * bi) - (cr * dr - ci * di),
-                (ar * bi + ai * br) - (cr * di + ci * dr),
-            )
-            for c in range(2):
-                cross = jnp.sum(jnp.sum(cacc[u, c], axis=1), axis=1, keepdims=True)
-                box_ref[c, u : u + 1, :] = along(box[c])
-                cross_ref[c, u : u + 1, :] = along(cross)
+        val = []
+        for one, two in ((first, first), (second, second), (first, second), (second, first)):
+            val.append([pick(tab[u, c], one, two) for c in range(2)])
+        (ar, ai), (br, bi), (cr, ci), (dr, di) = val
+        box = (
+            (ar * br - ai * bi) - (cr * dr - ci * di),
+            (ar * bi + ai * br) - (cr * di + ci * dr),
+        )
+        for c in range(2):
+            cross = jnp.sum(jnp.sum(cacc[u, c], axis=1), axis=1, keepdims=True)
+            out_ref[0, c, u : u + 1, :] = along(box[c])
+            out_ref[1, c, u : u + 1, :] = along(cross)
 
     def all_of(sem, count):
         ref = abuf_r.at[pl.ds(0, count)]
@@ -346,87 +344,91 @@
 
     chunks_out(0)
     chunks_out(1)
+    go(1, 1, 2)
+    go(0, 17, 18)
+    prepare()
+    go(1, 13)
+    go(1, 17, 18)
+    got(1, 2)
+    go(1, 6)
+    got(1, 1)
+    go(1, 5)
+    choose(0)
+    choose(1)
     go(0, 1, 2)
-    go(1, 1, 2)
-    prepare()
+    go(0, 9, 10)
     go(0, 13)
+    go(0, 0)
+    spread(0)
+    go(0, 21)
+    go(1, 0)
+    go(1, 9, 10)
     got(0, 2)
     go(0, 6)
     got(0, 1)
     go(0, 5)
-    got(1, 2)
-    go(1, 6)
-    choose(0)
-    got(1, 1)
-    go(1, 5)
-    choose(1)
-    go(1, 13)
-    go(1, 0)
-    go(1, 9, 10)
-    go(0, 9, 10)
-    spread(0)
+    spread(1)
     go(1, 21)
-    go(0, 21)
-    go(0, 0)
-    go(0, 17, 18)
-    go(1, 17, 18)
-    got(1, 10)
-    go(1, 12)
-    go(1, 15)
-    got(1, 9)
-    go(1, 11)
-    go(1, 14)
-    spread(1)
-    c_msg(0, 0).wait_recv()
-    c_msg(0, 4).start()
-    c_msg(0, 1).wait_recv()
-    c_msg(0, 5).start()
     got(0, 10)
     go(0, 15)
     go(0, 12)
+    got(0, 9)
+    go(0, 14)
+    got(0, 0)
+    go(0, 3, 20)
+    go(0, 11)
+    got(0, 17, 18)
+    chain(0, s, s_left, s_right)
+    c_msg(0, 0).wait_recv()
+    c_msg(0, 4).start()
+    got(1, 10)
+    go(1, 15)
+    c_msg(0, 1).wait_recv()
+    c_msg(0, 5).start()
+    go(1, 12)
+    got(1, 9)
+    go(1, 11)
+    got(0, 21)
+    go(0, 4, 19)
+    c_msg(0, 3).wait_recv()
+    k_msg(0, 2).start()
+    got(1, 17, 18)
+    chain(1, s, s_left, s_right)
+    go(1, 14)
+    c_msg(0, 2).wait_recv()
+    k_msg(0, 1).start()
+    c_msg(1, 1).wait_recv()
+    c_msg(1, 5).start()
+    c_msg(1, 0).wait_recv()
+    c_msg(1, 4).start()
     got(1, 0)
     go(1, 3, 20)
-    got(0, 9)
-    go(0, 14)
-    go(0, 11)
-    c_msg(0, 3).wait_recv()
-    k_msg(0, 2).start()
-    c_msg(0, 2).wait_recv()
-    k_msg(0, 1).start()
+    c_msg(1, 2).wait_recv()
+    k_msg(1, 1).start()
+    c_msg(1, 3).wait_recv()
+    k_msg(1, 2).start()
     got(1, 21)
     go(1, 4, 19)
-    got(0, 17, 18)
-    chain(0, s, s_left, s_right)
-    c_msg(1, 0).wait_recv()
-    c_msg(1, 4).start()
-    c_msg(1, 1).wait_recv()
-    c_msg(1, 5).start()
-    got(0, 21)
-    go(0, 4, 19)
-    got(1, 17, 18)
-    chain(1, s, s_left, s_right)
-    got(1, 13, 5, 6, 11, 12)
-    chain(1, s_par, s_opp)
+    got(0, 3)
+    go(0, 7)
     c_msg(0, 4).wait_recv()
     k_msg(0, 3).start()
     c_msg(0, 5).wait_recv()
     k_msg(0, 4).start()
-    got(0, 0)
-    go(0, 3, 20)
-    c_msg(1, 2).wait_recv()
-    k_msg(1, 1).start()
-    c_msg(1, 3).wait_recv()
-    k_msg(1, 2).start()
-    go(1, 16)
-    got(1, 3)
-    go(1, 7)
+    got(0, 13, 5, 6, 11, 12)
+    chain(0, s_par, s_opp)
+    c_msg(1, 5).wait_recv()
+    k_msg(1, 4).start()
     c_msg(1, 4).wait_recv()
     k_msg(1, 3).start()
-    c_msg(1, 5).wait_recv()
-    k_msg(1, 4).start()
-    got(0, 13, 5, 6, 11, 12)
-    chain(0, s_par, s_opp)
+    got(1, 13, 5, 6, 11, 12)
+    chain(1, s_par, s_opp)
+    go(1, 16)
     go(0, 16)
+    got(0, 4)
+    go(0, 8)
+    got(0, 19, 14, 20, 15)
+    chain(0, other(s_left), other(s_right))
     k_msg(0, 0).wait_recv()
     k_msg(0, 1).wait_recv()
     k_msg(0, 2).wait_recv()
@@ -443,25 +445,16 @@
     loops(0, s)
     loops(0, s_left)
     loops(0, s_right)
-    got(1, 4)
+    loops(0, other(s_left))
+    loops(0, other(s_right))
+    got(1, 3, 19, 14, 4, 20, 15)
+    chain(1, other(s_left), other(s_right))
+    go(1, 7)
     go(1, 8)
-    got(1, 19, 14, 20, 15)
-    chain(1, other(s_left), other(s_right))
-    got(0, 4)
-    go(0, 8)
     loops(0, s_par)
     loops(0, s_opp)
-    got(0, 3)
-    go(0, 7)
     loops(1, s_par)
     loops(1, s_opp)
-    got(0, 19, 14, 20, 15)
-    chain(0, other(s_left), other(s_right))
-    loops(0, other(s_left))
-    loops(0, other(s_right))
-    got(1, 7, 8, 16)
-    chain(1, other(s_opp))
-    loops(1, other(s_opp))
     loops(1, other(s_left))
     loops(1, other(s_right))
     got(0, 7, 8, 16)
@@ -476,6 +469,10 @@
     crossed(0, 5)
     crossed(0, 6)
     crossed(0, 7)
+    finish(0)
+    got(1, 7, 8, 16)
+    chain(1, other(s_opp))
+    loops(1, other(s_opp))
     trace_table(1)
     crossed(1, 0)
     crossed(1, 1)
@@ -485,7 +482,7 @@
     crossed(1, 5)
     crossed(1, 6)
     crossed(1, 7)
-    finish()
+    finish(1)
 
     for h in range(2):
         a_out[h].wait()
@@ -505,14 +502,11 @@
     sm = pl.BlockSpec(memory_space=pltpu.SMEM)
     hbm = pl.BlockSpec(memory_space=pl.ANY)
     dma = pltpu.SemaphoreType.DMA
-    boxes, crossed = pl.pallas_call(
+    both = pl.pallas_call(
         kernel,
-        out_shape=(
-            jax.ShapeDtypeStruct((2, 2, 8), F32),
-            jax.ShapeDtypeStruct((2, 2, 8), F32),
-        ),
+        out_shape=jax.ShapeDtypeStruct((2, 2, 2, 8), F32),
         in_specs=[sm, sm, hbm, hbm],
-        out_specs=(vm, vm),
+        out_specs=vm,
         scratch_shapes=[
             pltpu.VMEM((2, 8, 2, N, N), BF),
             pltpu.VMEM((2, 2, N, N), F32),
@@ -546,7 +540,7 @@
         ),
         name="diagrams",
     )(source_times, pair_index.T, elementals, perambulators)
-    return tuple(v.transpose(0, 2, 1)[:, :, None, :] for v in (boxes, crossed))
+    return tuple(v.transpose(0, 2, 1)[:, :, None, :] for v in (both[0], both[1]))
 
 
 def solution(mesh):

time: 54.9 us -> 52.9 us (0.964)
  Pallas kernels: 52.2 us -> 50.9 us
  local copies, waits for them, and re-layouts: 1.89 us -> 1.26 us
    pallas_call x1, Pallas kernels: 52.2 us -> 50.9 us  [local(): pl.pallas_call(kernel, out_shape=jax.ShapeDtypeStruct((2, 2, 2, 8), F32),...]
    unnamed x6 -> x1, local copies, waits for them, and re-layouts: 1.89 us -> 1.26 us
where the time goes in v4:
time: 52.9 us; the launch traced here: 52.8 us
  Pallas kernels  50.9 us (96%)
  local copies, waits for them, and re-layouts  1.26 us (2%)
  between operations  0.64 us (1%)
    pallas_call x1, Pallas kernels, local(): pl.pallas_call(kernel, out_shape=jax.ShapeDtypeStruct((2, 2, 2, 8), F32),...  50.9 us
    unnamed x1, local copies, waits for them, and re-layouts  1.26 us

profile of v4, /device:TPU:1, one launch (start us, length us, event | category | flops | bytes accessed | tf_op | source)
XLA Modules:
  0.0 52.8 jit_solution(3569765503960267279)
XLA Ops:
  0.6 50.9 %diagrams.1 = f32[2,2,2,8]{3,2,1,0:T(2,128)} custom-call(s32[8]{0:T(128)} %times.1, s32[2,8]{1,0:T(2,128)} %bitcast.17, bf16[2,1,2,256,256]{4,3,2,1,0:T(8,128)(2,1)} %e_in.1, f32[1,2,2,256,256]{4,3,2,1,0:T(8,128)} %p_in.1), custom_call_target="tpu_custom_call" | custom-call | tf_op jit(solution)/shard_map/diagrams/pallas_call | solution.py:505
  51.5 1.3 %slice_bitcast_fusion = (f32[2,8,1,2]{1,3,2,0:T(2,128)}, f32[2,8,1,2]{1,3,2,0:T(2,128)}) fusion(f32[2,2,2,8]{3,2,1,0:T(2,128)} %diagrams.1), kind=kLoop, calls=%fused_computation | loop fusion | bytes 512

commit v5 on v4

--- a/solution.py
+++ b/solution.py
@@ -447,10 +447,10 @@
     loops(0, s_right)
     loops(0, other(s_left))
     loops(0, other(s_right))
-    got(1, 3, 19, 14, 4, 20, 15)
+    got(1, 3, 4)
+    go(1, 7, 8)
+    got(1, 19, 14, 20, 15)
     chain(1, other(s_left), other(s_right))
-    go(1, 7)
-    go(1, 8)
     loops(0, s_par)
     loops(0, s_opp)
     loops(1, s_par)
@@ -470,6 +470,18 @@
     crossed(0, 6)
     crossed(0, 7)
     finish(0)
+    for h in range(2):
+        a_out[h].wait()
+        b_out[h].wait()
+        for j in range(6):
+            c_msg(h, j).wait_send()
+        for j in range(5):
+            k_msg(h, j).wait_send()
+    late = (7, 8, 16)
+    for t in range(2):
+        for j in range(22):
+            if j not in late:
+                e_msg(t, j).wait_send()
     got(1, 7, 8, 16)
     chain(1, other(s_opp))
     loops(1, other(s_opp))
@@ -484,17 +496,9 @@
     crossed(1, 7)
     finish(1)
 
-    for h in range(2):
-        a_out[h].wait()
-        b_out[h].wait()
     for t in range(2):
-        for j in range(22):
+        for j in late:
             e_msg(t, j).wait_send()
-    for h in range(2):
-        for j in range(6):
-            c_msg(h, j).wait_send()
-        for j in range(5):
-            k_msg(h, j).wait_send()
 
 
 def local(elementals, perambulators, source_times, pair_index):

time: 52.9 us -> 52.9 us (level)
  no operation moved by 1% of the time
where the time goes in v5:
time: 52.9 us; the launch traced here: 52.7 us
  Pallas kernels  50.8 us (96%)
  local copies, waits for them, and re-layouts  1.26 us (2%)
  between operations  0.64 us (1%)
    pallas_call x1, Pallas kernels, local(): pl.pallas_call(kernel, out_shape=jax.ShapeDtypeStruct((2, 2, 2, 8), F32),...  50.8 us
    unnamed x1, local copies, waits for them, and re-layouts  1.26 us

profile of v5, /device:TPU:1, one launch (start us, length us, event | category | flops | bytes accessed | tf_op | source)
XLA Modules:
  0.0 52.7 jit_solution(18385056883710224477)
XLA Ops:
  0.6 50.8 %diagrams.1 = f32[2,2,2,8]{3,2,1,0:T(2,128)} custom-call(s32[8]{0:T(128)} %times.1, s32[2,8]{1,0:T(2,128)} %bitcast.17, bf16[2,1,2,256,256]{4,3,2,1,0:T(8,128)(2,1)} %e_in.1, f32[1,2,2,256,256]{4,3,2,1,0:T(8,128)} %p_in.1), custom_call_target="tpu_custom_call" | custom-call | tf_op jit(solution)/shard_map/diagrams/pallas_call | solution.py:509
  51.4 1.3 %slice_bitcast_fusion = (f32[2,8,1,2]{1,3,2,0:T(2,128)}, f32[2,8,1,2]{1,3,2,0:T(2,128)}) fusion(f32[2,2,2,8]{3,2,1,0:T(2,128)} %diagrams.1), kind=kLoop, calls=%fused_computation | loop fusion | bytes 512
